TPU v7x, 256 devices: a whole 4x4x8 slice. The times are simulated.
256 devices in a mesh: gx: 16 (over z_hi, x, core), gy: 16 (over z_lo, y).
Axes of the slice: x: 4, y: 4, z: 8 (z_hi: 2, z_lo: 4; z = z_hi * 4 + z_lo), core: 2. Of those that a mesh axis runs over, the one named last changes fastest.
Arguments:
- node_feats: bfloat16 [262144, 128], P(('gx', 'gy')), may hold values from -6 to 6
- radial: bfloat16 [8, 32, 262144], P(None, None, ('gx', 'gy')), may hold values from -3 to 3
- neighbours: int32 [32, 262144], P(None, ('gx', 'gy')), may hold values from 0 to 8255, as said below
- nbr_count: int32 [262144], P(('gx', 'gy')), may hold values from 8 to 32, as said below
- domain_count: int32 [256], P(('gx', 'gy')), may hold values from 256 to 1024, as said below
- base_cells: int32 [3, 262144], P(None, ('gx', 'gy')), may hold values from 0 to 255, as said below
- spline_weights: float32 [3, 4, 262144], P(None, None, ('gx', 'gy')), as said below
- w_proj: bfloat16 [2, 128, 128], replicated, may hold values from -0.5 to 0.5
- w_radial: bfloat16 [2, 8, 128], replicated, may hold values from -2 to 2
- w_mix: bfloat16 [2, 128, 128], replicated, may hold values from -0.5 to 0.5
- w_charge: bfloat16 [128], replicated, may hold values from -0.5 to 0.5
- green_kernel: float32 [256, 256, 256], P(None, 'gx', 'gy'), may hold values from 1 to 200, as said below
Outputs:
- charges: float32 [262144], P(('gx', 'gy'))
- atom_potential: float32 [262144], P(('gx', 'gy'))
- potential_grid: float32 [256, 256, 256], P('gx', 'gy')
Inputs may be any that keep to these rules, and one draw needn't show every extreme that they name: `neighbours`: an entry is r * 1024 + t (see the steps). With r = 4 (the atom's own domain, slot s), t - s lies in -128 .. 127, and t is below that domain's count if s is. Atoms of slot s < 256 may also name other domains, by the band s // 64: band 0 names r with offset -1 along gx (any offset along gy) and t from 64 to 127; band 1 names offset +1 along gx (any along gy) and t below 64; band 2 names offset (0, -1) and t from 192 to 255; band 3 names offset (0, +1) and t from 128 to 191. Other atoms name only their own domain. Slots at or past nbr_count hold entries of the same kind. `nbr_count`: slots k below the count are live. `domain_count`: the present atoms of a domain fill its first slots. `base_cells`: row 0 lies in 1 to 16, row 1 in 1 to 16, row 2 in 0 to 255. `spline_weights`: for each dimension and atom, the four cubic B-spline weights of one fraction u in [0, 1): (1-u)^3/6, (3u^3-6u^2+4)/6, (-3u^3+3u^2+3u+1)/6, u^3/6. `green_kernel`: the value at wave number k equals the value at (-k) mod 256, taken along all three dimensions.
All inputs are finite; a program needn't handle non-finite values.
Results may differ from a plain program's by a relative error of at most 0.0075.
Values may be sent and summed in bfloat16 or wider, within the bound.
A program may use at most 64 MiB of HBM per device.

v0:
```python
import math

import jax
import jax.numpy as jnp
import ml_dtypes
import numpy as np
from jax import lax
from jax.experimental import pallas as pl
from jax.experimental.pallas import tpu as pltpu
from jax.sharding import PartitionSpec as P

K = 32
L = 2


MESH = pl.DeviceIdType.MESH
TN = (((0,), (0,)), ((), ()))
NT = (((1,), (1,)), ((), ()))
NN = (((1,), (0,)), ((), ()))


def dot(a, b, dims=NN):
    return lax.dot_general(a, b, dims, preferred_element_type=jnp.float32)


def ring(index, step, count):
    return lax.rem(index + step + count, count)


def message_stage(
    enter,
    idle,
    feats_ref,
    radial_ref,
    nbr_ref,
    count_ref,
    fill_ref,
    proj_ref,
    filt_ref,
    mix_ref,
    charge_w_ref,
    charges_ref,
    state,
    table,
    rows_out,
    rows_in,
    head_a,
    head_b,
    pick,
    filt_k,
    total,
    send_sem,
    recv_sem,
):
    px, py = lax.axis_index("gx"), lax.axis_index("gy")
    num_x = num_y = 16
    peers = [(dx, dy) for dx in (-1, 0, 1) for dy in (-1, 0, 1) if (dx, dy) != (0, 0)]
    code = nbr_ref[...]
    direction, slot = code // 1024, code % 1024
    lane = lax.broadcasted_iota(jnp.int32, (K, 1024), 1)
    live = lax.broadcasted_iota(jnp.int32, (K, 1024), 0) < count_ref[...]
    block = lane // 128
    near = slot - jnp.maximum(block - 1, 0) * 128
    far = jnp.where(
        direction < 3,
        192 + direction * 64 + slot,
        jnp.where(
            direction > 5,
            64 + direction * 64 + slot,
            jnp.where(direction == 3, 192 + slot, 320 + slot),
        ),
    )
    named = jnp.where(live, jnp.where(direction == 4, near, far), -8192).astype(jnp.float32)
    for b in range(8):
        pick[:, b, :] = named[:, b * 128 : (b + 1) * 128]

    state[...] = jnp.transpose(feats_ref[...].astype(jnp.float32))
    row_id = lax.broadcasted_iota(jnp.int32, (128, 128), 0).astype(jnp.bfloat16)
    one, zero = jnp.ones((128, 128), jnp.bfloat16), jnp.zeros((128, 128), jnp.bfloat16)
    basis_k = lax.broadcasted_iota(jnp.int32, (128, 8 * K), 1) % K

    def onehot(k, begin, groups):
        row = pick[k, begin // 128 : begin // 128 + 1, :]
        parts = [
            jnp.where(row_id == jnp.broadcast_to((row - 128.0 * g).astype(jnp.bfloat16), (128, 128)), one, zero)
            for g in range(groups)
        ]
        return jnp.concatenate(parts, axis=0)

    def messages(group, tables):
        begin = group * 256
        radial = radial_ref[:, begin : begin + 256]
        total[...] = jnp.zeros_like(total)

        for k in range(0, K, 2):
            filters = dot(filt_k[k * 128 : k * 128 + 256, :], radial)
            for half, (source, groups) in enumerate(tables):
                at = begin + 128 * half
                hot = jnp.concatenate([onehot(k, at, groups), onehot(k + 1, at, groups)], axis=1)
                got = dot(source(), hot)
                lanes = slice(128 * half, 128 * half + 128)
                total[:, lanes] += (
                    got[:, :128] * filters[:128, lanes] + got[:, 128:] * filters[128:, lanes]
                )
        return (total[...] * (1.0 / math.sqrt(K))).astype(jnp.bfloat16)

    for layer in range(L):
        spread = jnp.concatenate(
            [jnp.broadcast_to(filt_ref[layer, b : b + 1], (K, 128)) for b in range(8)], axis=0
        )
        spread = jnp.transpose(spread.astype(jnp.float32))
        for k in range(K):
            filt_k[k * 128 : (k + 1) * 128, :] = jnp.where(basis_k == k, spread, 0.0).astype(jnp.bfloat16)
        proj = proj_ref[layer]
        first = dot(proj, state[:, :256].astype(jnp.bfloat16), TN).astype(jnp.bfloat16)
        rows_out[layer] = jnp.transpose(first.astype(jnp.float32)).astype(jnp.bfloat16)
        if layer == 0:
            enter()
        copies = []
        for dx, dy in peers:
            if dx == 1:
                band, land = 1, 1 - dy
            elif dx == -1:
                band, land = 0, 4 - dy
            elif dy == 1:
                band, land = 3, 6
            else:
                band, land = 2, 7
            copies.append(
                pltpu.make_async_remote_copy(
                    src_ref=rows_out.at[layer, pl.ds(band * 64, 64)],
                    dst_ref=rows_in.at[layer, pl.ds(land * 64, 64)],
                    send_sem=send_sem.at[layer, land],
                    recv_sem=recv_sem.at[layer, land],
                    device_id=(ring(px, dx, num_x), ring(py, dy, num_y)),
                    device_id_type=MESH,
                )
            )
            copies[-1].start()
        table[:, :256] = first
        table[:, 256:] = dot(proj, state[:, 256:].astype(jnp.bfloat16), TN).astype(jnp.bfloat16)

        def update(group, tables):
            begin = group * 256
            u = messages(group, tables)
            mixed = dot(mix_ref[layer], u, TN)
            lanes = slice(begin, begin + 256)
            state[:, lanes] = (
                (state[:, lanes] + mixed / (1.0 + jnp.exp(-mixed))).astype(jnp.bfloat16).astype(jnp.float32)
            )

        def window(block):
            low = max(block - 1, 0) * 128
            high = min(block + 2, 8) * 128
            return (lambda: table[:, low:high]), (high - low) // 128

        for group in (1, 2, 3):
            update(group, [window(2 * group), window(2 * group + 1)])
        idle[layer]()
        for copy in copies:
            copy.wait()
        far_rows = jnp.transpose(rows_in[layer].astype(jnp.float32)).astype(jnp.bfloat16)
        head_a[:, :256] = table[:, :256]
        head_a[:, 256:] = far_rows[:, :384]
        head_b[:, :384] = table[:, :384]
        head_b[:, 384:] = far_rows[:, 384:]
        update(0, [((lambda: head_a[...]), 5), ((lambda: head_b[...]), 4)])
    charge = dot(jnp.broadcast_to(charge_w_ref[...], (8, 128)), state[...].astype(jnp.bfloat16))[0:1]
    inside = lax.broadcasted_iota(jnp.int32, (1, 1024), 1) < fill_ref[0]
    charges_ref[...] = jnp.where(inside, charge, 0.0)


def split(values):
    high = values.astype(jnp.bfloat16)
    return high, (values - high.astype(jnp.float32)).astype(jnp.bfloat16)


def np_split(values):
    high = values.astype(ml_dtypes.bfloat16)
    return high, (values - high.astype(np.float64)).astype(ml_dtypes.bfloat16)


def mesh_tables():
    ids = np.arange(256)
    angles = 2.0 * np.pi * (ids[:, None] * ids[None, :] % 256) / 256
    waves = np.concatenate([np.cos(angles), np.sin(angles)], axis=0)
    column, slot = np.arange(16)[:, None], np.arange(8)[None, :]
    kz = (16 * column + slot + (column >= 8)).reshape(128)
    turn = 2.0 * np.pi * (kz[:, None] * ids[None, :] % 256) / 256
    ahead = np.stack([np.cos(turn), -np.sin(turn)])
    back = 2.0 * ahead
    ahead[0, 0], ahead[1, 0] = 1.0, 1.0 - 2.0 * (ids % 2)
    back[0, 0], back[1, 0] = ahead[0, 0], ahead[1, 0]
    back = back / 256.0**3
    return (
        *np_split(waves),
        *np_split(ahead.reshape(256, 256)),
        *np_split(back.reshape(256, 256)),
    )


def regroup(parts):
    group = lax.broadcasted_iota(jnp.int32, parts[0].shape, 1) // 16
    parts = list(parts)
    for step in (1, 2, 4):
        low = (group & step) == 0
        for i in range(8):
            if i & step == 0:
                a, b = parts[i], parts[i | step]
                parts[i] = jnp.where(low, a, pltpu.roll(b, 16 * step, 1))
                parts[i | step] = jnp.where(low, pltpu.roll(a, 128 - 16 * step, 1), b)
    return parts


def swap_groups(values):
    row = lax.broadcasted_iota(jnp.int32, values.shape, 1)
    group = lax.broadcasted_iota(jnp.int32, values.shape, 2) // 16
    for step in (1, 2, 4):
        row_high, group_high = (row & step) != 0, (group & step) != 0
        if step == 4:
            moved = pltpu.roll(pltpu.roll(values, 4, 1), 64, 2)
        else:
            up = pltpu.roll(pltpu.roll(values, 8 - step, 1), 16 * step, 2)
            down = pltpu.roll(pltpu.roll(values, step, 1), 128 - 16 * step, 2)
            moved = jnp.where(row_high, down, up)
        values = jnp.where(row_high == group_high, values, moved)
    return values


def turned(values, step):
    return jnp.concatenate([values[step:], values[:step]], axis=0)


def fold_edges(edge):
    before, after = turned(edge, -1), turned(edge, 1)
    row = lax.broadcasted_iota(jnp.int32, edge.shape, 1)
    return [
        jnp.concatenate(
            [
                jnp.where(row < 2, pltpu.roll(before, step, 1), 0.0),
                jnp.where(row >= 6, pltpu.roll(after, step, 1), 0.0),
            ],
            axis=1,
        )
        for step in (6, 2)
    ]


def edges_of(real, imag):
    row = lax.broadcasted_iota(jnp.int32, (16, 8, 128), 1)
    ends = [
        pltpu.roll(part, step, 1)
        for values, step in ((real, 2), (imag, 6))
        for part in (turned(values, -1)[:, 8:], turned(values, 1)[:, :8])
    ]
    return jnp.where(
        row < 2, ends[0], jnp.where(row < 4, ends[1], jnp.where(row < 6, ends[2], ends[3]))
    )


def tile(low, high=None):
    high = jnp.zeros_like(low) if high is None else high
    return jnp.concatenate([low, high], axis=low.ndim - 2).astype(jnp.bfloat16)


def profile(cells, base, weights):
    total = jnp.zeros(cells.shape, jnp.float32)
    for offset in range(4):
        total = total + jnp.where(cells == base[offset], weights[offset], 0.0)
    return total


def mesh_stage(
    charges_ref,
    fill_ref,
    base_ref,
    spline_ref,
    green_ref,
    wave_h,
    wave_l,
    ahead_h,
    ahead_l,
    back_h,
    back_l,
    atom_ref,
    grid_ref,
    plane,
    prof_h,
    prof_l,
    z_out,
    z_in,
    y_out,
    y_in,
    x_out,
    x_in,
    v_out,
    v_in,
    shared,
    shared_edge,
    green,
    green_out,
    green_in,
    send_sem,
    recv_sem,
):
    count = 16
    px, py = lax.axis_index("gx"), lax.axis_index("gy")
    def remote(source, target, stage, index, where):
        return pltpu.make_async_remote_copy(
            src_ref=source,
            dst_ref=target,
            send_sem=send_sem.at[stage, index],
            recv_sem=recv_sem.at[stage, index],
            device_id=where,
            device_id_type=MESH,
        )

    def exchange(make):
        def start(d, carry):
            make(d).start()
            return carry

        lax.fori_loop(1, count, start, 0)

    def arrive(make):
        def wait(d, carry):
            make(d).wait()
            return carry

        lax.fori_loop(1, count, wait, 0)

    def column_copy(out, into, stage):
        def make(d):
            to = ring(py, d, count)
            return remote(out.at[to], into.at[py], stage, d, (px, to))

        return make

    def row_copy(out, into, stage, layers):
        def make(d):
            to = ring(px, d, count)
            return remote(out.at[to, layers], into.at[px, layers], stage, d, (to, py))

        return make

    main, extra = pl.ds(0, 3), pl.ds(3, 2)

    def green_copy():
        return remote(green_out, green_in, 8, 0, (px, 0))

    def rows(dim):
        base = base_ref[dim : dim + 1, :]
        cells = [base + offset for offset in range(4)]
        if dim == 2:
            cells = [jnp.where(c >= 256, c - 256, c) for c in cells]
        return cells, [spline_ref[dim, o : o + 1, :] for o in range(4)]

    def lines_of_atoms():
        z_cells = lax.broadcasted_iota(jnp.int32, (256, 1024), 0)
        high, low = split(profile(z_cells, *rows(2)))
        prof_h[...] = high
        prof_l[...] = low
        slots = [green_ref[:, i, :] for i in range(9)]
        green_out[...] = slots[0]
        picked = [jnp.where(py < 8, slots[i], slots[i + 1]) for i in range(8)]
        green[...] = jnp.transpose(jnp.concatenate(picked, axis=0))

    def planes_of_atoms():
        sixteen = lax.broadcasted_iota(jnp.int32, (16, 1024), 0)
        eight = lax.broadcasted_iota(jnp.int32, (8, 1024), 0)
        edge = jnp.where(eight < 2, eight, eight + 16)
        in_x, in_y = (profile(sixteen + 2, *rows(dim)) for dim in (0, 1))
        edge_x, edge_y = (profile(edge, *rows(dim)) for dim in (0, 1))
        for y in range(16):
            plane[16 * y : 16 * y + 16, :] = in_y[y : y + 1, :] * in_x
        for y in range(16):
            plane[256 + 8 * y : 264 + 8 * y, :] = in_y[y : y + 1, :] * edge_x
        for i in range(4):
            plane[384 + 16 * i : 400 + 16 * i, :] = edge_y[i : i + 1, :] * in_x
            plane[448 + 8 * i : 456 + 8 * i, :] = edge_y[i : i + 1, :] * edge_x

    def run():
        high, low = split(plane[...] * charges_ref[...])
        spread = dot(high, prof_h[...], NT) + dot(low, prof_h[...], NT) + dot(high, prof_l[...], NT)
        edges = spread[256:]
        edges = [
            tile(edges[:128].reshape(16, 8, 256)).reshape(256, 256),
            tile(edges[128:192]),
            tile(tile(edges[192:].reshape(4, 8, 256)).reshape(64, 256)),
        ]
        edges = jnp.concatenate(edges, axis=0)
        high, low = split(spread[:256])

        lines = dot(ahead_h[...], high, NT) + dot(ahead_l[...], high, NT) + dot(ahead_h[...], low, NT)
        halves = [
            swap_groups(lines[:, 128 * half : 128 * half + 128].reshape(32, 8, 128)) for half in (0, 1)
        ]
        halves = jnp.concatenate(halves, axis=1).astype(jnp.bfloat16)
        z_out[:, 0] = halves[:16]
        z_out[:, 1] = halves[16:]
        lines = dot(ahead_h[...], edges, NT) + dot(ahead_l[...], edges, NT)
        real, imag = lines[:128], lines[128:]
        sides = real[:, :256] + pltpu.roll(imag[:, :256], 4, 1)
        ends = real[:, 256:384] + pltpu.roll(imag[:, 256:384], 64, 1)
        corners = real[:, 384:] + pltpu.roll(imag[:, 384:], 4, 1)
        pieces = [
            swap_groups(part.reshape(16, 8, 128))
            for part in (sides[:, :128], sides[:, 128:], ends, corners)
        ]
        z_out[:, 2] = tile(pieces[0], pieces[1])
        z_out[:, 3] = tile(pieces[2], pieces[3])
        make = column_copy(z_out, z_in, 2)
        exchange(make)

        @pl.when(py == 8)
        def _():
            green_copy().start()

        z_in[pl.ds(py, 1)] = z_out[pl.ds(py, 1)]
        arrive(make)

        cos_h, sin_h = wave_h[:256], wave_h[256:]
        cos_l, sin_l = wave_l[:256], wave_l[256:]
        ends = z_in[:, 3].astype(jnp.float32)
        adds = [*fold_edges(ends[:, :8]), fold_edges(ends[:, 8:])[0]]
        both = jnp.concatenate(
            [(z_in[:, i].astype(jnp.float32) + adds[i]).reshape(256, 128) for i in range(3)], axis=1
        )
        both = jnp.transpose(both).astype(jnp.bfloat16)
        c = dot(both, cos_h) + dot(both, cos_l)
        s = dot(both, sin_h) + dot(both, sin_l)
        apart = (lax.broadcasted_iota(jnp.int32, (128, 256), 0) < 16) & (py == 0)
        real = c[:128] + jnp.where(apart, 0.0, s[128:256])
        imag = jnp.where(apart, 0.0, c[128:256]) - s[:128]

        c_edge, s_edge = (v[256:].reshape(8, 16, 256)[:, :8] for v in (c, s))
        c_swap, s_swap = pltpu.roll(c_edge, 4, 1), pltpu.roll(s_edge, 4, 1)
        top = lax.broadcasted_iota(jnp.int32, (8, 8, 256), 1) < 4
        apart = (lax.broadcasted_iota(jnp.int32, (8, 8, 256), 0) == 0) & (py == 0)
        edge = jnp.where(
            top,
            c_edge + jnp.where(apart, 0.0, s_swap),
            jnp.where(apart, 0.0, c_edge) - s_swap,
        )

        def to_slots(values, layer):
            for half in (0, 1):
                lanes = slice(128 * half, 128 * half + 128)
                done = regroup([v[:, lanes] for v in values])
                for i in range(8):
                    whole = done[i].shape[0] == 16
                    y_out[8 * half + i, layer] = done[i].astype(jnp.bfloat16) if whole else tile(done[i])

        to_slots([real[16 * i : 16 * i + 16] for i in range(8)], 0)
        to_slots([imag[16 * i : 16 * i + 16] for i in range(8)], 1)
        to_slots([edge[i] for i in range(8)], 2)
        make = row_copy(y_out, y_in, 3, main)
        exchange(make)
        y_in[pl.ds(px, 1), 0:3] = y_out[pl.ds(px, 1), 0:3]

        @pl.when(py == 0)
        def _():
            blank = jnp.zeros((16, 256), jnp.float32)
            to_slots([c[128:144], -s[128:144]] + [blank] * 6, 3)
            to_slots([jnp.where(top[0], c_swap[0], -s_edge[0])] + [blank[:8]] * 7, 4)
            exchange(row_copy(y_out, y_in, 4, extra))
            y_in[pl.ds(px, 1), 3:5] = y_out[pl.ds(px, 1), 3:5]

        arrive(make)

        def forward_x(values):
            return dot(cos_h, values) + dot(cos_l, values), dot(sin_h, values) + dot(sin_l, values)

        def inverse_x(values):
            high, low = split(values)
            return (
                dot(cos_h, high) + dot(cos_l, high) + dot(cos_h, low),
                dot(sin_h, high) + dot(sin_l, high) + dot(sin_h, low),
            )

        adds = fold_edges(y_in[:, 2].astype(jnp.float32)[:, :8])
        c, s = forward_x(
            jnp.concatenate(
                [(y_in[:, i].astype(jnp.float32) + adds[i]).reshape(256, 128) for i in range(2)], axis=1
            ).astype(jnp.bfloat16)
        )
        real = (c[:, :128] + s[:, 128:]) * green[...]
        imag = (c[:, 128:] - s[:, :128]) * green[...]
        c, s = inverse_x(jnp.concatenate([real, imag], axis=1))
        real = (c[:, :128] - s[:, 128:]).reshape(16, 16, 128)
        imag = (c[:, 128:] + s[:, :128]).reshape(16, 16, 128)
        x_out[:, 0] = real.astype(jnp.bfloat16)
        x_out[:, 1] = imag.astype(jnp.bfloat16)
        x_out[:, 2] = tile(edges_of(real, imag))
        make = row_copy(x_out, x_in, 5, main)
        exchange(make)
        x_in[pl.ds(px, 1), 0:3] = x_out[pl.ds(px, 1), 0:3]

        @pl.when(py == 0)
        def _():
            arrive(row_copy(y_out, y_in, 4, extra))
            green_copy().wait_recv()
            first = lax.broadcasted_iota(jnp.int32, (256, 128), 1) < 16
            adds = fold_edges(y_in[:, 4].astype(jnp.float32)[:, :8])
            last = y_in[:, 3].astype(jnp.float32) + adds[0] + pltpu.roll(adds[1], 16, 2)
            c, s = forward_x(last.reshape(256, 128).astype(jnp.bfloat16))
            kernel = jnp.transpose(
                jnp.concatenate([green_in[...], jnp.zeros((112, 256), jnp.float32)], axis=0)
            )
            real = (c + pltpu.roll(s, 112, 1)) * kernel
            imag = (pltpu.roll(c, 112, 1) - s) * kernel
            c, s = inverse_x(real + pltpu.roll(imag, 16, 1))
            real = jnp.where(first, c - pltpu.roll(s, 112, 1), 0.0)
            imag = jnp.where(first, pltpu.roll(c, 112, 1) + s, 0.0)
            x_out[:, 3] = (real + pltpu.roll(imag, 16, 1)).astype(jnp.bfloat16).reshape(16, 16, 128)
            x_out[:, 4] = tile(edges_of(real.reshape(16, 16, 128), imag.reshape(16, 16, 128)))
            back_copy = row_copy(x_out, x_in, 6, extra)
            exchange(back_copy)
            x_in[pl.ds(px, 1), 3:5] = x_out[pl.ds(px, 1), 3:5]

        @pl.when(py == 8)
        def _():
            green_copy().wait_send()

        arrive(make)

        def to_rows(layer, count=16):
            halves = [
                regroup([x_in[8 * half + i, layer].astype(jnp.float32)[:count] for i in range(8)])
                for half in (0, 1)
            ]
            return [jnp.concatenate([halves[0][i], halves[1][i]], axis=1) for i in range(8)]

        real, imag, edge = to_rows(0), to_rows(1), to_rows(2, 8)
        shared[0] = real[0]
        shared[1] = imag[0]
        shared_edge[...] = edge[0]

        @pl.when(py == 0)
        def _():
            arrive(row_copy(x_out, x_in, 6, extra))
            last = to_rows(3)
            shared[0] = -last[1]
            shared[1] = last[0]
            last = pltpu.roll(to_rows(4, 8)[0], 4, 0)
            shared_edge[...] = jnp.where(top[0], -last, last)

        a = jnp.concatenate(real, axis=0).astype(jnp.bfloat16)
        b = jnp.concatenate(imag, axis=0).astype(jnp.bfloat16)
        a_too = jnp.concatenate([shared[0], *real[1:]], axis=0).astype(jnp.bfloat16)
        b_too = jnp.concatenate([shared[1], *imag[1:]], axis=0).astype(jnp.bfloat16)
        real = dot(cos_h, a, NT) + dot(cos_l, a, NT) - dot(sin_h, b, NT) - dot(sin_l, b, NT)
        imag = dot(cos_h, b_too, NT) + dot(cos_l, b_too, NT) + dot(sin_h, a_too, NT) + dot(sin_l, a_too, NT)
        sides = []
        for first in (edge[0], shared_edge[...]):
            rows = jnp.concatenate([tile(v) for v in [first, *edge[1:]]], axis=0)
            sides.append(
                (
                    dot(cos_h, rows, NT) + dot(cos_l, rows, NT),
                    dot(sin_h, rows, NT) + dot(sin_l, rows, NT),
                )
            )
        within = lax.broadcasted_iota(jnp.int32, (256, 128), 1) % 16
        sides = jnp.where(
            within < 4,
            sides[0][0] - pltpu.roll(sides[0][1], 124, 1),
            sides[1][0] + pltpu.roll(sides[1][1], 4, 1),
        )
        sides = jnp.where(within < 8, sides, 0.0).reshape(16, 16, 128)
        real, imag = real.reshape(16, 16, 128), imag.reshape(16, 16, 128)
        v_out[:, 0] = real.astype(jnp.bfloat16)
        v_out[:, 1] = imag.astype(jnp.bfloat16)
        v_out[:, 2] = sides.astype(jnp.bfloat16)
        v_out[:, 3] = tile(edges_of(real, imag), edges_of(sides, sides))
        make = column_copy(v_out, v_in, 7)
        exchange(make)
        v_in[pl.ds(py, 1)] = v_out[pl.ds(py, 1)]
        arrive(make)

        def to_lines(values):
            return swap_groups(values).reshape(-1, 128)

        got = jnp.concatenate([v_in[:, 0], v_in[:, 1]], axis=0).astype(jnp.float32)
        lines = jnp.concatenate([to_lines(got[:, :8]), to_lines(got[:, 8:])], axis=1).astype(jnp.bfloat16)
        grid = dot(lines, back_h[...], TN) + dot(lines, back_l[...], TN)
        for y in range(16):
            grid_ref[:, y, :] = grid[16 * y : 16 * y + 16]
        got = jnp.concatenate([v_in[:, 2], v_in[:, 3]], axis=0).astype(jnp.float32)
        sides = jnp.concatenate([to_lines(got[:16, :8]), to_lines(got[:16, 8:])], axis=1)
        ends, corners = to_lines(got[16:, :8]), to_lines(got[16:, 8:])
        lines = jnp.concatenate(
            [
                jnp.concatenate([sides, ends, corners], axis=1),
                jnp.concatenate(
                    [pltpu.roll(sides, 252, 1), pltpu.roll(ends, 64, 1), pltpu.roll(corners, 124, 1)],
                    axis=1,
                ),
            ],
            axis=0,
        ).astype(jnp.bfloat16)
        edges = dot(lines, back_h[...], TN) + dot(lines, back_l[...], TN)

        values = jnp.concatenate(
            [
                grid,
                edges[:256].reshape(16, 16, 256)[:, :8].reshape(128, 256),
                edges[256:320],
                edges[384:448].reshape(4, 16, 256)[:, :8].reshape(32, 256),
            ],
            axis=0,
        )
        high, low = split(values)
        sampled = dot(high, prof_h[...]) + dot(low, prof_h[...]) + dot(high, prof_l[...])
        total = jnp.sum(sampled * plane[...], axis=0, keepdims=True)
        inside = lax.broadcasted_iota(jnp.int32, (1, 1024), 1) < fill_ref[0]
        atom_ref[...] = jnp.where(inside, total, 0.0)

    return lines_of_atoms, planes_of_atoms, run


def step_kernel(*refs):
    far, fill_ref, outs = refs[:17], refs[17], refs[18:21]
    near, load_sem, refs = refs[21:38], refs[38], refs[39:]
    message_scratch, mesh_scratch = refs[:11], refs[11:]
    loads = [
        pltpu.make_async_copy(source, target, load_sem.at[i])
        for i, (source, target) in enumerate(zip(far, near, strict=True))
    ]
    for load in loads:
        load.start()
    feats_ref, nbr_ref, count_ref, radial_ref, *weights, charge_w_ref = near[:8]
    message_in = (feats_ref, radial_ref, nbr_ref, count_ref, fill_ref, *weights, charge_w_ref)
    count = 16
    px, py = lax.axis_index("gx"), lax.axis_index("gy")
    barrier = pltpu.get_barrier_semaphore()

    def greet(d, carry):
        for where in ((ring(px, d, count), py), (px, ring(py, d, count))):
            pl.semaphore_signal(barrier, inc=1, device_id=where, device_id_type=MESH)
        return carry

    lax.fori_loop(1, count, greet, 0)
    for dx in (-1, 1):
        for dy in (-1, 1):
            pl.semaphore_signal(
                barrier,
                inc=1,
                device_id=(ring(px, dx, count), ring(py, dy, count)),
                device_id_type=MESH,
            )
    lines_of_atoms, planes_of_atoms, run = mesh_stage(
        outs[0], fill_ref, *near[8:], *outs[1:], *mesh_scratch
    )

    def first_idle():
        for load in loads[8:]:
            load.wait()
        lines_of_atoms()

    for load in loads[:8]:
        load.wait()
    message_stage(
        lambda: pl.semaphore_wait(barrier, 34),
        (first_idle, planes_of_atoms),
        *message_in,
        outs[0],
        *message_scratch,
    )
    run()


def hand_on(*refs):
    copies = [pltpu.make_async_copy(refs[i], refs[3 + i], refs[6].at[i]) for i in range(3)]
    for copy in copies:
        copy.start()
    for copy in copies:
        copy.wait()


def shards(
    node_feats,
    radial,
    neighbours,
    nbr_count,
    domain_count,
    base_cells,
    spline_weights,
    w_proj,
    w_radial,
    w_mix,
    w_charge,
    green_kernel,
):
    vmem = pl.BlockSpec(memory_space=pltpu.VMEM)
    bf16, f32 = jnp.bfloat16, jnp.float32
    far = [
        node_feats,
        neighbours,
        nbr_count.reshape(1, 1024),
        radial.reshape(8 * K, 1024),
        w_proj,
        w_radial,
        w_mix,
        w_charge.reshape(1, 128),
        base_cells,
        spline_weights,
        jnp.transpose(green_kernel, (1, 2, 0)),
        *(jnp.asarray(table) for table in mesh_tables()),
    ]
    charges, atom_potential, potential = pl.pallas_call(
        step_kernel,
        out_shape=(
            jax.ShapeDtypeStruct((1, 1024), f32),
            jax.ShapeDtypeStruct((1, 1024), f32),
            jax.ShapeDtypeStruct((16, 16, 256), f32),
        ),
        in_specs=[pl.BlockSpec(memory_space=pltpu.HBM)] * 17
        + [pl.BlockSpec(memory_space=pltpu.SMEM)],
        out_specs=(vmem, vmem, vmem),
        scratch_shapes=[
            *(pltpu.VMEM(array.shape, array.dtype) for array in far),
            pltpu.SemaphoreType.DMA((17,)),
            pltpu.VMEM((128, 1024), f32),
            pltpu.VMEM((128, 1024), bf16),
            pltpu.VMEM((L, 256, 128), bf16),
            pltpu.VMEM((L, 512, 128), bf16),
            pltpu.VMEM((128, 640), bf16),
            pltpu.VMEM((128, 512), bf16),
            pltpu.VMEM((K, 8, 128), f32),
            pltpu.VMEM((K * 128, 8 * K), bf16),
            pltpu.VMEM((128, 256), f32),
            pltpu.SemaphoreType.DMA((L, 8)),
            pltpu.SemaphoreType.DMA((L, 8)),
            pltpu.VMEM((480, 1024), f32),
            pltpu.VMEM((256, 1024), bf16),
            pltpu.VMEM((256, 1024), bf16),
            *[pltpu.VMEM((16, 4, 16, 128), bf16)] * 2,
            *[pltpu.VMEM((16, 5, 16, 128), bf16)] * 4,
            *[pltpu.VMEM((16, 4, 16, 128), bf16)] * 2,
            pltpu.VMEM((2, 16, 256), f32),
            pltpu.VMEM((8, 256), f32),
            pltpu.VMEM((256, 128), f32),
            pltpu.VMEM((16, 256), f32),
            pltpu.VMEM((16, 256), f32),
            pltpu.SemaphoreType.DMA((9, 16)),
            pltpu.SemaphoreType.DMA((9, 16)),
        ],
        compiler_params=pltpu.CompilerParams(
            collective_id=0, has_side_effects=True, vmem_limit_bytes=56 * 1024 * 1024
        ),
        name="potential_step",
    )(
        *far,
        domain_count,
    )
    results = (charges, atom_potential, potential)
    charges, atom_potential, potential = pl.pallas_call(
        hand_on,
        out_shape=tuple(jax.ShapeDtypeStruct(array.shape, f32) for array in results),
        in_specs=[pl.BlockSpec(memory_space=pl.ANY)] * 3,
        out_specs=[pl.BlockSpec(memory_space=pl.ANY)] * 3,
        scratch_shapes=[pltpu.SemaphoreType.DMA((3,))],
        name="hand_on",
    )(*results)
    return (charges.reshape(1024), atom_potential.reshape(1024), potential)


def solution(mesh):
    return jax.shard_map(
        shards,
        mesh=mesh,
        in_specs=(
            P(("gx", "gy"), None),
            P(None, None, ("gx", "gy")),
            P(None, ("gx", "gy")),
            P(("gx", "gy")),
            P(("gx", "gy")),
            P(None, ("gx", "gy")),
            P(None, None, ("gx", "gy")),
            P(),
            P(),
            P(),
            P(),
            P(None, "gx", "gy"),
        ),
        out_specs=(P(("gx", "gy")), P(("gx", "gy")), P("gx", "gy", None)),
        check_vma=False,
    )
```

profile of v0, /device:TPU:1, one launch (start us, length us, event | category | flops | bytes accessed | tf_op | source)
XLA Modules:
  0.0 80.5 jit_solution(2659129519648185713)
XLA Ops:
  1.3 69.7 %potential_step.1 = (f32[1,1024]{1,0:T(1,128)}, f32[1,1024]{1,0:T(1,128)}, f32[16,16,256]{2,1,0:T(8,128)}) custom-call(bf16[1024,128]{1,0:T(8,128)(2,1)} %refs_0_.1, s32[32,1024]{1,0:T(8,128)} %refs_1_.1, s32[1,1024]{1,0:T(1,128)} %bitcast.8, bf16[256,1024]{1,0:T(8,128)(2,1)} %bitcast.6, bf16[2,128,128]{2,1,0:T(8,128)(2,1)} %refs_4_.1, ...), custom_call_target="tpu_custom_call" | custom-call | tf_op jit(solution)/shard_map/potential_step/pallas_call | solution.py:710
  71.0 9.3 %hand_on.1 = (f32[1,1024]{1,0:T(1,128)}, f32[1,1024]{1,0:T(1,128)}, f32[16,16,256]{2,1,0:T(8,128)}) custom-call(f32[1,1024]{1,0:T(1,128)} %get-tuple-element.9.refs_0_, f32[1,1024]{1,0:T(1,128)} %get-tuple-element.10.refs_1_, f32[16,16,256]{2,1,0:T(8,128)} %get-tuple-element.11.refs_2_), custom_call_target="tpu_custom_call" | custom-call | tf_op jit(solution)/shard_map/hand_on/pallas_call | solution.py:757
where the time goes:
time: 81.6 us; the launch traced here: 80.5 us
  Pallas kernels  79.1 us (97%)
  between operations  1.47 us (2%)
    pallas_call x1, Pallas kernels, shards(): pl.pallas_call(step_kernel, out_shape=(jax.ShapeDtypeStruct((1, 1024), f3...  69.7 us
    pallas_call x1, Pallas kernels, shards(): pl.pallas_call(hand_on, out_shape=tuple((jax.ShapeDtypeStruct(array.shape...  9.32 us

commit v1 on v0

--- a/solution.py
+++ b/solution.py
@@ -670,11 +670,8 @@
 
 
 def hand_on(*refs):
-    copies = [pltpu.make_async_copy(refs[i], refs[3 + i], refs[6].at[i]) for i in range(3)]
-    for copy in copies:
-        copy.start()
-    for copy in copies:
-        copy.wait()
+    for source, target in zip(refs[:3], refs[3:], strict=True):
+        target[...] = source[...]
 
 
 def shards(
@@ -757,9 +754,8 @@
     charges, atom_potential, potential = pl.pallas_call(
         hand_on,
         out_shape=tuple(jax.ShapeDtypeStruct(array.shape, f32) for array in results),
-        in_specs=[pl.BlockSpec(memory_space=pl.ANY)] * 3,
-        out_specs=[pl.BlockSpec(memory_space=pl.ANY)] * 3,
-        scratch_shapes=[pltpu.SemaphoreType.DMA((3,))],
+        in_specs=[vmem] * 3,
+        out_specs=[vmem] * 3,
         name="hand_on",
     )(*results)
     return (charges.reshape(1024), atom_potential.reshape(1024), potential)

time: 81.6 us -> 73.8 us (0.904)
  Pallas kernels: 79.1 us -> 71.4 us
    pallas_call x1, Pallas kernels: 9.32 us -> 1.68 us  [shards(): pl.pallas_call(hand_on, out_shape=tuple((jax.ShapeDtypeStruct(array.shape...]
where the time goes in v1:
time: 73.8 us; the launch traced here: 72.7 us
  Pallas kernels  71.4 us (97%)
  between operations  1.29 us (2%)
    pallas_call x1, Pallas kernels, shards(): pl.pallas_call(step_kernel, out_shape=(jax.ShapeDtypeStruct((1, 1024), f3...  69.7 us
    pallas_call x1, Pallas kernels, shards(): pl.pallas_call(hand_on, out_shape=tuple((jax.ShapeDtypeStruct(array.shape...  1.68 us

profile of v1, /device:TPU:1, one launch (start us, length us, event | category | flops | bytes accessed | tf_op | source)
XLA Modules:
  0.0 72.7 jit_solution(3200148971586617028)
XLA Ops:
  1.3 69.7 %potential_step.1 = (f32[1,1024]{1,0:T(1,128)}, f32[1,1024]{1,0:T(1,128)}, f32[16,16,256]{2,1,0:T(8,128)}) custom-call(bf16[1024,128]{1,0:T(8,128)(2,1)} %refs_0_.1, s32[32,1024]{1,0:T(8,128)} %refs_1_.1, s32[1,1024]{1,0:T(1,128)} %bitcast.8, bf16[256,1024]{1,0:T(8,128)(2,1)} %bitcast.6, bf16[2,128,128]{2,1,0:T(8,128)(2,1)} %refs_4_.1, ...), custom_call_target="tpu_custom_call" | custom-call | tf_op jit(solution)/shard_map/potential_step/pallas_call | solution.py:707
  71.0 1.7 %hand_on.1 = (f32[1,1024]{1,0:T(1,128)}, f32[1,1024]{1,0:T(1,128)}, f32[16,16,256]{2,1,0:T(8,128)}) custom-call(f32[1,1024]{1,0:T(1,128)} %get-tuple-element.9.refs_0_, f32[1,1024]{1,0:T(1,128)} %get-tuple-element.10.refs_1_, f32[16,16,256]{2,1,0:T(8,128)} %get-tuple-element.11.refs_2_), custom_call_target="tpu_custom_call" | custom-call | tf_op jit(solution)/shard_map/hand_on/pallas_call | solution.py:754

commit v2 on v1

--- a/solution.py
+++ b/solution.py
@@ -317,7 +317,7 @@
 
     def exchange(make):
         def start(d, carry):
-            make(d).start()
+            make(lax.rem(d + 3, count - 1) + 1).start()
             return carry
 
         lax.fori_loop(1, count, start, 0)

time: 73.8 us -> 74.8 us (1.014)
  Pallas kernels: 71.4 us -> 73.1 us
    pallas_call x1, Pallas kernels: 69.7 us -> 71.4 us  [shards(): pl.pallas_call(step_kernel, out_shape=(jax.ShapeDtypeStruct((1, 1024), f3...]
where the time goes in v2:
time: 74.8 us; the launch traced here: 74.4 us
  Pallas kernels  73.1 us (98%)
  between operations  1.29 us (2%)
    pallas_call x1, Pallas kernels, shards(): pl.pallas_call(step_kernel, out_shape=(jax.ShapeDtypeStruct((1, 1024), f3...  71.4 us
    pallas_call x1, Pallas kernels, shards(): pl.pallas_call(hand_on, out_shape=tuple((jax.ShapeDtypeStruct(array.shape...  1.68 us

profile of v2, /device:TPU:1, one launch (start us, length us, event | category | flops | bytes accessed | tf_op | source)
XLA Modules:
  0.0 74.4 jit_solution(7075968507549581127)
XLA Ops:
  1.3 71.4 %potential_step.1 = (f32[1,1024]{1,0:T(1,128)}, f32[1,1024]{1,0:T(1,128)}, f32[16,16,256]{2,1,0:T(8,128)}) custom-call(bf16[1024,128]{1,0:T(8,128)(2,1)} %refs_0_.1, s32[32,1024]{1,0:T(8,128)} %refs_1_.1, s32[1,1024]{1,0:T(1,128)} %bitcast.8, bf16[256,1024]{1,0:T(8,128)(2,1)} %bitcast.6, bf16[2,128,128]{2,1,0:T(8,128)(2,1)} %refs_4_.1, ...), custom_call_target="tpu_custom_call" | custom-call | tf_op jit(solution)/shard_map/potential_step/pallas_call | solution.py:707
  72.7 1.7 %hand_on.1 = (f32[1,1024]{1,0:T(1,128)}, f32[1,1024]{1,0:T(1,128)}, f32[16,16,256]{2,1,0:T(8,128)}) custom-call(f32[1,1024]{1,0:T(1,128)} %get-tuple-element.9.refs_0_, f32[1,1024]{1,0:T(1,128)} %get-tuple-element.10.refs_1_, f32[16,16,256]{2,1,0:T(8,128)} %get-tuple-element.11.refs_2_), custom_call_target="tpu_custom_call" | custom-call | tf_op jit(solution)/shard_map/hand_on/pallas_call | solution.py:754
